TPU v7x, 512 devices: a whole 4x8x8 slice. The times are simulated.
512 devices in a mesh: dp: 64 (over z_hi, y, core), tensor: 8 (over z_lo, x).
Axes of the slice: x: 4, y: 8, z: 8 (z_hi: 4, z_lo: 2; z = z_hi * 2 + z_lo), core: 2. Of those that a mesh axis runs over, the one named last changes fastest.
Arguments:
- tokens: bfloat16 [32768, 8192], P('dp', 'tensor'), may hold values from -6 to 6
- value_weight: bfloat16 [8192, 1024], P('tensor', 'dp'), may hold values from -0.0625 to 0.0625
- adapter_down_weights: bfloat16 [8, 8192, 64], P(None, 'tensor'), may hold values from -0.0625 to 0.0625
- adapter_up_weights: bfloat16 [8, 64, 1024], P(None, None, 'tensor'), may hold values from -0.75 to 0.75
- value_gradient: bfloat16 [32768, 1024], P(('dp', 'tensor')), may hold values from -12 to 12
- block_adapter_index: int32 [256, 1], replicated, may hold values from 0 to 7
- block_live_rows: int32 [256], replicated, may hold values from 1 to 128
Outputs:
- values_out: bfloat16 [32768, 1024], P(('dp', 'tensor'))
- input_gradient: bfloat16 [32768, 8192], P('dp', 'tensor')
- grad_a: float32 [8, 8192, 64], P(None, 'tensor')
- grad_b: float32 [8, 64, 1024], P(None, None, 'tensor')
Inputs may be any that keep to these rules, and one draw needn't show every extreme that they name: `block_adapter_index`: every adapter names at least one block.
All inputs are finite; a program needn't handle non-finite values.
Results may differ from a plain program's by a relative error of at most 0.02.
Values may be sent and summed in bfloat16 or wider, within the bound.
No kernel may reach another device: no remote copies, remote signals or barrier semaphores. Data moves between devices by JAX's collectives and lax.ppermute only.
A program may use at most 64 MiB of HBM per device.

v0:
```python
import jax
import jax.numpy as jnp
from jax import lax
from jax.sharding import PartitionSpec as P

BLK = 128
ADAPTER_SCALE = 2.0


def shards(
    tokens,
    value_weight,
    adapter_down_weights,
    adapter_up_weights,
    value_gradient,
    block_adapter_index,
    block_live_rows,
):
    local_rows = tokens.shape[0]
    tensor_size = lax.axis_size("tensor")
    own_rows = local_rows // tensor_size
    data_index = lax.axis_index("dp")
    tensor_index = lax.axis_index("tensor")
    adapter_count = adapter_down_weights.shape[0]
    local_width = tokens.shape[1]
    rank_columns = adapter_down_weights.shape[2]
    head_columns = adapter_up_weights.shape[2]
    local_blocks = local_rows // BLK
    all_ids = block_adapter_index[:, 0]
    block_indices = lax.dynamic_slice_in_dim(all_ids, data_index * local_blocks, local_blocks)
    block_fill = lax.dynamic_slice_in_dim(block_live_rows, data_index * local_blocks, local_blocks)
    adapter_range = jnp.arange(adapter_count, dtype=jnp.int32)
    block_onehot = (block_indices[:, None] == adapter_range[None, :]).astype(jnp.float32)
    complete_up_weight = lax.all_gather(adapter_up_weights, "tensor", axis=2, tiled=True)
    up_flat = complete_up_weight.reshape(adapter_count * rank_columns, complete_up_weight.shape[2])
    selected_down_weight = adapter_down_weights[block_indices]
    token_block_rows = tokens.reshape(local_blocks, BLK, local_width)
    reduced_part = jnp.einsum(
        "cpe,cev->cpv", token_block_rows, selected_down_weight, preferred_element_type=jnp.float32
    )
    reduced = lax.psum(reduced_part.astype(jnp.bfloat16), "tensor")
    w_full = lax.all_gather(value_weight, "dp", axis=1, tiled=True)
    base_own = lax.psum_scatter(
        jnp.dot(tokens, w_full, preferred_element_type=jnp.float32).astype(jnp.bfloat16),
        "tensor",
        scatter_dimension=0,
        tiled=True,
    ).astype(jnp.float32)
    row_index = tensor_index * own_rows + jnp.arange(own_rows, dtype=jnp.int32)
    row_block = row_index // BLK
    row_ids = block_indices[row_block]
    row_onehot = row_ids[:, None] == adapter_range[None, :]
    reduced_own = lax.dynamic_slice_in_dim(
        reduced.reshape(local_rows, rank_columns), tensor_index * own_rows, own_rows, 0
    )
    spread = (row_onehot[:, :, None].astype(jnp.bfloat16) * reduced_own[:, None, :]).reshape(
        own_rows, adapter_count * rank_columns
    )
    update = jnp.dot(spread, up_flat, preferred_element_type=jnp.float32)
    values_out = (base_own + ADAPTER_SCALE * update).astype(jnp.bfloat16)
    live_rows = row_index % BLK < block_fill[row_block]
    masked = jnp.where(live_rows[:, None], value_gradient, jnp.zeros_like(value_gradient))
    projected = jnp.einsum("kc,mc->km", masked, up_flat, preferred_element_type=jnp.float32)
    grad_low = jnp.sum(
        projected.reshape(own_rows, adapter_count, rank_columns)
        * row_onehot[:, :, None].astype(jnp.float32),
        axis=1,
    ).astype(jnp.bfloat16)
    whole_grad, whole_low = (
        lax.all_gather(masked, "tensor", axis=0, tiled=True),
        lax.all_gather(grad_low, "tensor", axis=0, tiled=True),
    )
    lowrank_block_rows = whole_low.reshape(local_blocks, BLK, rank_columns)
    base_backward = jnp.einsum("kc,dc->kd", whole_grad, w_full, preferred_element_type=jnp.float32)
    adapter_backward = jnp.einsum(
        "sly,say->sla", lowrank_block_rows, selected_down_weight, preferred_element_type=jnp.float32
    ).reshape(local_rows, local_width)
    input_gradient = (base_backward + ADAPTER_SCALE * adapter_backward).astype(jnp.bfloat16)
    down_terms = jnp.einsum(
        "xgj,xgi->xji", token_block_rows, lowrank_block_rows, preferred_element_type=jnp.float32
    )
    down_local = jnp.einsum(
        "ba,bdr->adr", block_onehot, down_terms, precision=lax.Precision.HIGHEST
    )
    grad_cols = lax.dynamic_slice_in_dim(
        whole_grad, tensor_index * head_columns, head_columns, 1
    ).reshape(local_blocks, BLK, head_columns)
    up_terms = jnp.einsum("bkr,bkc->brc", reduced, grad_cols, preferred_element_type=jnp.float32)
    up_local = jnp.einsum("ba,brc->arc", block_onehot, up_terms, precision=lax.Precision.HIGHEST)
    all_onehot = (all_ids[:, None] == adapter_range[None, :]).astype(jnp.float32)
    tallies = jnp.sum(all_onehot * block_live_rows[:, None].astype(jnp.float32), axis=0)
    factor = ADAPTER_SCALE / tallies
    down_sum, up_sum = lax.psum((down_local, up_local), "dp")
    grad_a = down_sum * factor[:, None, None]
    grad_b = up_sum * factor[:, None, None]
    return (values_out, input_gradient, grad_a, grad_b)


def solution(mesh):
    return jax.shard_map(
        shards,
        mesh=mesh,
        in_specs=(
            P("dp", "tensor"),
            P("tensor", "dp"),
            P(None, "tensor", None),
            P(None, None, "tensor"),
            P(("dp", "tensor"), None),
            P(),
            P(),
        ),
        out_specs=(
            P(("dp", "tensor"), None),
            P("dp", "tensor"),
            P(None, "tensor", None),
            P(None, None, "tensor"),
        ),
        check_vma=False,
    )
```

profile of v0, /device:TPU:8, one launch (start us, length us, event | category | flops | bytes accessed | tf_op | source)
XLA Modules:
  0.0 890.9 jit_solution(14993300499443759841)
XLA Ops:
  7.2 0.0 copy-start
  7.2 0.0 all-gather.6.cloned.1.call-start
  7.2 0.7 all-gather.6.cloned.1.call-update
  7.9 0.0 all-gather.8.cloned.1.call-start
  8.0 0.8 dynamic_slice.17
  8.7 0.6 fusion.26
  9.3 2.6 fusion.21
  11.9 1.6 broadcast_select_fusion
  13.6 0.0 copy-start.2
  13.6 0.0 all-gather.8.cloned.1.call-update
  13.6 0.0 all-reduce.4.cloned.1.call-start
  13.6 0.7 fusion.25
  14.4 1.8 gather_fusion
  16.2 0.0 copy-done
  16.2 1.1 fusion.5
  17.3 0.0 all-reduce.4.cloned.1.call-update
  17.3 0.0 all-gather.4.cloned.1.call-start
  17.4 0.5 all-gather.4.cloned.1.call-update
  17.9 0.0 all-reduce.6.cloned.1.call-start
  18.0 0.6 fusion.27
  18.6 2.6 fusion.23
  21.2 36.1 %all-gather.6.cloned.1.call-done = bf16[8,64,1024]{2,1,0:T(8,128)(2,1)} async-done(((bf16[8,64,128]{2,1,0:T(8,128)(2,1)}), bf16[8,64,1024]{2,1,0:T(8,128)(2,1)}) %all-gather.6.cloned.1.call-update) | async-done | bytes 1048592 | tf_op jit(solution)/shard_map/all_gather | solution.py:34
  57.3 0.0 copy-done.2
  57.3 1.9 fusion.4
  59.1 28.3 %all_gather.15 = bf16[512,64]{1,0:T(8,128)(2,1)S(1)} all-gather(bf16[64,64]{1,0:T(8,128)(2,1)S(1)} %fusion.4), channel_id=1, replica_groups=mesh['dp'=64,'tensor'=8] {'tensor'}, dimensions={0}, use_global_device_ids=true | all-gather | bytes 73728 | tf_op jit(solution)/shard_map/all_gather | solution.py:71
  87.4 18.4 %all-gather.8.cloned.1.call-done = bf16[512,1024]{1,0:T(8,128)(2,1)} async-done(((bf16[64,1024]{1,0:T(8,128)(2,1)}), bf16[512,1024]{1,0:T(8,128)(2,1)}) %all-gather.8.cloned.1.call-update) | async-done | bytes 1048592 | tf_op jit(solution)/shard_map/all_gather | solution.py:70
  105.7 0.9 constant_dynamic-slice_fusion
  106.7 85.2 %all-reduce.4.cloned.1.call-done = bf16[4,128,64]{1,2,0:T(8,128)(2,1)} async-done(((bf16[4,128,64]{1,2,0:T(8,128)(2,1)}), bf16[4,128,64]{1,2,0:T(8,128)(2,1)}) %all-reduce.4.cloned.1.call-update) | async-done | bytes 65552 | tf_op jit(solution)/shard_map/psum | solution.py:41
  191.8 1.0 fusion.28
  192.8 1.1 fusion.9
  193.9 0.4 convolution_bitcast_fusion
  194.3 3.2 fusion.6
  197.5 0.0 all-reduce.6.cloned.1.call-update
  197.5 0.0 copy-start.7
  197.5 0.0 copy-start.6
  197.6 0.0 copy-start.4
  197.6 0.0 reduce-scatter.2.cloned.1.call-start
  197.6 81.2 %all-gather.4.cloned.1.call-done = bf16[1024,1024]{0,1:T(8,128)(2,1)} async-done(((bf16[1024,16]{0,1:T(8,128)(2,1)}), bf16[1024,1024]{0,1:T(8,128)(2,1)}) %all-gather.4.cloned.1.call-update) | async-done | bytes 2097168 | tf_op jit(solution)/shard_map/all_gather | solution.py:42
  278.9 3.9 convolution_convert_fusion
  282.7 0.0 copy-start.5
  282.7 0.0 reduce-scatter.2.cloned.1.call-update
  282.7 0.0 copy-done.7
  282.8 0.0 copy-done.6
  282.8 0.1 select_reduce_fusion
  282.9 0.0 copy-done.4
  282.9 0.1 constant_dynamic-slice_fusion.1
  283.0 0.1 copy.28
  283.1 0.0 copy-start.8
  283.1 0.4 convolution_multiply_fusion
  283.5 0.4 copy-done.5
  283.9 0.8 copy-done.8
  284.8 2.2 fusion
  287.0 548.4 %all-reduce.6.cloned.1.call-done = (f32[8,1024,64]{1,0,2:T(8,128)}, f32[8,64,128]{2,0,1:T(8,128)}) async-done(((f32[8,1024,64]{1,0,2:T(8,128)}, f32[8,64,128]{2,0,1:T(8,128)}), (f32[8,1024,64]{1,0,2:T(8,128)}, f32[8,64,128]{2,0,1:T(8,128)})) %all-reduce.6.cloned.1.call-update) | async-done | bytes 2359312 | tf_op jit(solution)/shard_map/psum | solution.py:93
  835.4 1.8 broadcast_multiply_fusion
  837.3 0.0 copy-start.3
  837.3 0.0 copy-start.1
  837.3 2.5 copy.34
  839.8 0.0 copy-done.3
  839.8 0.1 broadcast_multiply_fusion.1
  839.9 0.8 copy.35
  840.7 41.4 %reduce-scatter.2.cloned.1.call-done = bf16[64,1024]{1,0:T(8,128)(2,1)} async-done(((bf16[512,1024]{1,0:T(8,128)(2,1)}), bf16[64,1024]{1,0:T(8,128)(2,1)}) %reduce-scatter.2.cloned.1.call-update) | async-done | bytes 131088 | tf_op jit(solution)/shard_map/reduce_scatter | solution.py:43
  882.1 0.0 copy-done.1
  882.1 2.0 fusion.3
  (5 shorter events, 0.0 us)
Async XLA Ops:
  7.2 9.0 %copy-start = (bf16[512,1024]{1,0:T(8,128)(2,1)S(1)}, bf16[512,1024]{1,0:T(8,128)(2,1)}, u32[]{:S(2)}) copy-start(bf16[512,1024]{1,0:T(8,128)(2,1)} %param.7) | copy-start | bytes 3145732
  7.2 50.1 %all-gather.6.cloned.1.call-start = ((), (), s32[]{:S(2)}) async-start(), calls=%async_computation.4 | async-start | bytes 1179648 | tf_op jit(solution)/shard_map/all_gather | solution.py:34
  7.9 97.8 %all-gather.8.cloned.1.call-start = ((), (), s32[]{:S(2)}) async-start(), calls=%async_computation.5 | async-start | bytes 1179648 | tf_op jit(solution)/shard_map/all_gather | solution.py:70
  13.6 43.7 %copy-start.2 = (bf16[64,1024]{1,0:T(8,128)(2,1)S(1)}, bf16[64,1024]{1,0:T(8,128)(2,1)}, u32[]{:S(2)}) copy-start(bf16[64,1024]{1,0:T(8,128)(2,1)} %broadcast_select_fusion) | copy-start | bytes 393220
  13.6 178.2 %all-reduce.4.cloned.1.call-start = ((), (), s32[]{:S(2)}) async-start(), calls=%async_computation.3 | async-start | bytes 131072 | tf_op jit(solution)/shard_map/psum | solution.py:41
  17.3 261.5 %all-gather.4.cloned.1.call-start = ((), (), s32[]{:S(2)}) async-start(), calls=%async_computation.1 | async-start | bytes 2129920 | tf_op jit(solution)/shard_map/all_gather | solution.py:42
  17.9 817.5 %all-reduce.6.cloned.1.call-start = ((), (), s32[]{:S(2)}) async-start(), calls=%async_computation.6 | async-start | bytes 4718592 | tf_op jit(solution)/shard_map/psum | solution.py:93
  197.5 85.2 %copy-start.7 = (s32[256]{0:T(256)S(1)}, s32[256]{0:T(256)}, u32[]{:S(2)}) copy-start(s32[256]{0:T(256)} %param.13) | copy-start | bytes 3076
  197.5 85.2 %copy-start.6 = (s32[256,1]{0,1:T(1,128)S(1)}, s32[256,1]{0,1:T(1,128)}, u32[]{:S(2)}) copy-start(s32[256,1]{0,1:T(1,128)} %param.12) | copy-start | bytes 3076
  197.6 85.4 %copy-start.4 = (bf16[4,128,64]{1,2,0:T(8,128)(2,1)S(1)}, bf16[4,128,64]{1,2,0:T(8,128)(2,1)}, u32[]{:S(2)}) copy-start(bf16[4,128,64]{1,2,0:T(8,128)(2,1)} %all-reduce.4.cloned.1.call-done) | copy-start | bytes 196612
  197.6 684.5 %reduce-scatter.2.cloned.1.call-start = ((), (), s32[]{:S(2)}) async-start(), calls=%async_computation.2 | async-start | bytes 1179648 | tf_op jit(solution)/shard_map/reduce_scatter | solution.py:43
  282.7 1.2 copy-start.5
  283.1 1.7 copy-start.8
  837.3 2.6 copy-start.3
  837.3 44.8 %copy-start.1 = (bf16[8,64,1024]{2,1,0:T(8,128)(2,1)S(1)}, bf16[8,64,1024]{2,1,0:T(8,128)(2,1)}, u32[]{:S(2)}) copy-start(bf16[8,64,1024]{2,1,0:T(8,128)(2,1)} %all-gather.6.cloned.1.call-done) | copy-start | bytes 3145732
Sparse Core Ops, SparseCore 0:
  10.0 47.1 all-gather.5
  59.9 45.7 all-gather.7
  109.2 82.5 all-reduce.3
  195.6 83.2 all-gather.3
  282.5 552.8 all-reduce.5
  838.1 43.9 reduce-scatter.1
where the time goes:
time: 891 us
  waiting for transfers between devices  812 us (91%)
  blocking collectives  28.3 us (3%)
  matrix products  17.1 us (2%)
  between operations  14.3 us (2%)
  other arithmetic  9.62 us (1%)
  local copies, waits for them, and re-layouts  9.44 us (1%)
    psum x1, waiting for transfers between devices, shards(): down_sum, up_sum = lax.psum((down_local, up_local), 'dp')  548 us
    psum x1, waiting for transfers between devices, shards(): reduced = lax.psum(reduced_part.astype(jnp.bfloat16), 'tensor')  85.2 us
    all_gather x1, waiting for transfers between devices, shards(): w_full = lax.all_gather(value_weight, 'dp', axis=1, tiled=True)  81.2 us
    reduce_scatter x1, waiting for transfers between devices, shards(): lax.psum_scatter(jnp.dot(tokens, w_full, preferred_element_type=jnp.float...  41.4 us
    all_gather x1, waiting for transfers between devices, shards(): lax.all_gather(adapter_up_weights, 'tensor', axis=2, tiled=True)  36.1 us
    all_gather x1, blocking collectives, shards(): lax.all_gather(grad_low, 'tensor', axis=0, tiled=True)  28.3 us
    all_gather x1, waiting for transfers between devices, shards(): lax.all_gather(masked, 'tensor', axis=0, tiled=True)  18.4 us
  transfers between devices with their start and end apart: 6, of which 6 were waited for; matrix products, arithmetic and copies ran while one was open for 4% of the time, Pallas kernels for 0%

commit v1 on v0

--- a/solution.py
+++ b/solution.py
@@ -5,6 +5,13 @@
 
 BLK = 128
 ADAPTER_SCALE = 2.0
+
+
+def apply_types(t0, chip_axis):
+    step_out = jnp.concatenate(
+        jax.lax.all_to_all(jnp.stack(jax.lax.axis_size(chip_axis) * [t0]), chip_axis, 0, 0), axis=1
+    )
+    return step_out
 
 
 def shards(
@@ -39,7 +46,7 @@
         "cpe,cev->cpv", token_block_rows, selected_down_weight, preferred_element_type=jnp.float32
     )
     reduced = lax.psum(reduced_part.astype(jnp.bfloat16), "tensor")
-    w_full = lax.all_gather(value_weight, "dp", axis=1, tiled=True)
+    w_full = apply_types(value_weight, "dp")
     base_own = lax.psum_scatter(
         jnp.dot(tokens, w_full, preferred_element_type=jnp.float32).astype(jnp.bfloat16),
         "tensor",

time: 891 us -> 856 us (0.961)
  waiting for transfers between devices: 812 us -> 759 us
  starting transfers between devices: 0.24 us -> 17.1 us
    all_gather x1 -> x0, waiting for transfers between devices: 81.2 us -> none  [shards(): w_full = lax.all_gather(value_weight, 'dp', axis=1, tiled=True)]
    all_gather x1, waiting for transfers between devices: 18.4 us -> 53.2 us  [shards(): lax.all_gather(masked, 'tensor', axis=0, tiled=True)]
    psum x1, waiting for transfers between devices: 85.2 us -> 57 us  [shards(): reduced = lax.psum(reduced_part.astype(jnp.bfloat16), 'tensor')]
    all_gather x1, waiting for transfers between devices: 36.1 us -> 61.2 us  [shards(): lax.all_gather(adapter_up_weights, 'tensor', axis=2, tiled=True)]
    all_to_all x0 -> x1, starting transfers between devices: none -> 16.9 us  [apply_types(): jax.lax.all_to_all(jnp.stack(jax.lax.axis_size(chip_axis) * [t0]), chip_a...]
  transfers between devices with their start and end apart: 6 -> 6, of which waited for: 6 -> 5; matrix products, arithmetic and copies ran while one was open for 4% -> 4% of each run, Pallas kernels for 0% -> 0%
where the time goes in v1:
time: 856 us
  waiting for transfers between devices  759 us (89%)
  blocking collectives  28.2 us (3%)
  matrix products  18.8 us (2%)
  starting transfers between devices  17.1 us (2%)
  between operations  14 us (2%)
  local copies, waits for them, and re-layouts  9.71 us (1%)
  other arithmetic  8.86 us (1%)
    psum x1, waiting for transfers between devices, shards(): down_sum, up_sum = lax.psum((down_local, up_local), 'dp')  546 us
    all_gather x1, waiting for transfers between devices, shards(): lax.all_gather(adapter_up_weights, 'tensor', axis=2, tiled=True)  61.2 us
    psum x1, waiting for transfers between devices, shards(): reduced = lax.psum(reduced_part.astype(jnp.bfloat16), 'tensor')  57 us
    all_gather x1, waiting for transfers between devices, shards(): lax.all_gather(masked, 'tensor', axis=0, tiled=True)  53.2 us
    reduce_scatter x1, waiting for transfers between devices, shards(): lax.psum_scatter(jnp.dot(tokens, w_full, preferred_element_type=jnp.float...  41.4 us
    all_gather x1, blocking collectives, shards(): lax.all_gather(grad_low, 'tensor', axis=0, tiled=True)  28.2 us
  transfers between devices with their start and end apart: 6, of which 5 were waited for; matrix products, arithmetic and copies ran while one was open for 4% of the time, Pallas kernels for 0%

profile of v1, /device:TPU:8, one launch (start us, length us, event | category | flops | bytes accessed | tf_op | source)
XLA Modules:
  0.0 855.8 jit_solution(738483759114783430)
XLA Ops:
  7.2 0.0 copy-start
  7.2 0.0 all-gather.3.cloned.1.call-start
  7.2 0.7 all-gather.3.cloned.1.call-update
  7.9 0.0 all-gather.5.cloned.1.call-start
  8.0 0.8 dynamic_slice.17
  8.7 0.6 fusion.26
  9.3 2.6 fusion.21
  11.9 1.6 broadcast_select_fusion
  13.6 0.0 all-gather.5.cloned.1.call-update
  13.6 2.3 stack.2
  15.9 0.0 copy-start.7
  15.9 0.0 copy-start.3
  15.9 16.9 %all-to-all-start = ((bf16[64,1024,16]{1,2,0:T(8,128)(2,1)}), bf16[64,1024,16]{1,2,0:T(8,128)(2,1)}, u32[]{:S(2)}, u32[]{:S(2)}) async-start(bf16[64,1024,16]{1,2,0:T(8,128)(2,1)} %stack.2), calls=%async_computation | async-start | bytes 4194304 | tf_op jit(solution)/shard_map/all_to_all | solution.py:12
  32.8 0.0 copy-start.2
  32.9 0.0 all-reduce.4.cloned.1.call-start
  32.9 0.0 copy-done.7
  32.9 0.1 fusion.25
  33.0 0.0 copy-done.3
  33.0 0.6 gather_fusion
  33.6 0.0 copy-done
  33.6 1.1 fusion.5
  34.7 0.0 all-reduce.4.cloned.1.call-update
  34.7 0.0 all-reduce.6.cloned.1.call-start
  34.8 0.6 fusion.27
  35.4 2.5 fusion.23
  37.9 61.2 %all-gather.3.cloned.1.call-done = bf16[8,64,1024]{2,1,0:T(8,128)(2,1)} async-done(((bf16[8,64,128]{2,1,0:T(8,128)(2,1)}), bf16[8,64,1024]{2,1,0:T(8,128)(2,1)}) %all-gather.3.cloned.1.call-update) | async-done | bytes 1048592 | tf_op jit(solution)/shard_map/all_gather | solution.py:41
  99.1 0.0 copy-done.2
  99.1 1.9 fusion.4
  100.9 53.2 %all-gather.5.cloned.1.call-done = bf16[512,1024]{1,0:T(8,128)(2,1)} async-done(((bf16[64,1024]{1,0:T(8,128)(2,1)}), bf16[512,1024]{1,0:T(8,128)(2,1)}) %all-gather.5.cloned.1.call-update) | async-done | bytes 1048592 | tf_op jit(solution)/shard_map/all_gather | solution.py:77
  154.1 0.9 constant_dynamic-slice_fusion
  155.0 28.2 %all_gather.11 = bf16[512,64]{1,0:T(8,128)(2,1)S(1)} all-gather(bf16[64,64]{1,0:T(8,128)(2,1)S(1)} %fusion.4), channel_id=1, replica_groups=mesh['dp'=64,'tensor'=8] {'tensor'}, dimensions={0}, use_global_device_ids=true | all-gather | bytes 73728 | tf_op jit(solution)/shard_map/all_gather | solution.py:78
  183.2 57.0 %all-reduce.4.cloned.1.call-done = bf16[4,128,64]{1,2,0:T(8,128)(2,1)} async-done(((bf16[4,128,64]{1,2,0:T(8,128)(2,1)}), bf16[4,128,64]{1,2,0:T(8,128)(2,1)}) %all-reduce.4.cloned.1.call-update) | async-done | bytes 65552 | tf_op jit(solution)/shard_map/psum | solution.py:48
  240.2 1.0 fusion.28
  241.2 1.1 fusion.9
  242.3 0.4 convolution_bitcast_fusion
  242.7 3.2 fusion.6
  245.9 0.0 all-reduce.6.cloned.1.call-update
  246.0 0.0 reduce-scatter.2.cloned.1.call-start
  246.0 0.0 all-to-all-done
  246.0 0.0 copy-start.8
  246.0 0.0 copy-start.5
  246.0 4.0 convolution_convert_fusion
  250.0 0.0 copy-start.6
  250.0 0.0 reduce-scatter.2.cloned.1.call-update
  250.0 0.0 copy-done.8
  250.0 0.1 select_reduce_fusion
  250.2 0.0 copy-done.5
  250.2 0.1 constant_dynamic-slice_fusion.1
  250.3 0.1 copy.29
  250.4 0.4 convolution_multiply_fusion
  250.8 0.4 copy-done.6
  251.2 3.8 fusion
  255.0 545.5 %all-reduce.6.cloned.1.call-done = (f32[8,1024,64]{1,0,2:T(8,128)}, f32[8,64,128]{2,0,1:T(8,128)}) async-done(((f32[8,1024,64]{1,0,2:T(8,128)}, f32[8,64,128]{2,0,1:T(8,128)}), (f32[8,1024,64]{1,0,2:T(8,128)}, f32[8,64,128]{2,0,1:T(8,128)})) %all-reduce.6.cloned.1.call-update) | async-done | bytes 2359312 | tf_op jit(solution)/shard_map/psum | solution.py:100
  800.6 1.8 broadcast_multiply_fusion
  802.4 0.0 copy-start.4
  802.4 0.0 copy-start.1
  802.5 2.5 copy.35
  805.0 0.0 copy-done.4
  805.0 0.1 broadcast_multiply_fusion.1
  805.1 0.8 copy.36
  805.8 41.4 %reduce-scatter.2.cloned.1.call-done = bf16[64,1024]{1,0:T(8,128)(2,1)} async-done(((bf16[512,1024]{1,0:T(8,128)(2,1)}), bf16[64,1024]{1,0:T(8,128)(2,1)}) %reduce-scatter.2.cloned.1.call-update) | async-done | bytes 131088 | tf_op jit(solution)/shard_map/reduce_scatter | solution.py:50
  847.3 0.0 copy-done.1
  847.3 2.0 fusion.3
  (5 shorter events, 0.0 us)
Async XLA Ops:
  7.2 26.4 %copy-start = (bf16[512,1024]{1,0:T(8,128)(2,1)S(1)}, bf16[512,1024]{1,0:T(8,128)(2,1)}, u32[]{:S(2)}) copy-start(bf16[512,1024]{1,0:T(8,128)(2,1)} %param.7) | copy-start | bytes 3145732
  7.2 91.9 %all-gather.3.cloned.1.call-start = ((), (), s32[]{:S(2)}) async-start(), calls=%async_computation.4 | async-start | bytes 1179648 | tf_op jit(solution)/shard_map/all_gather | solution.py:41
  7.9 146.2 %all-gather.5.cloned.1.call-start = ((), (), s32[]{:S(2)}) async-start(), calls=%async_computation.5 | async-start | bytes 1179648 | tf_op jit(solution)/shard_map/all_gather | solution.py:77
  15.9 17.0 %copy-start.7 = (s32[256,1]{0,1:T(1,128)S(1)}, s32[256,1]{0,1:T(1,128)}, u32[]{:S(2)}) copy-start(s32[256,1]{0,1:T(1,128)} %param.12) | copy-start | bytes 3076
  15.9 17.1 %copy-start.3 = (bf16[8,1024,64]{1,2,0:T(8,128)(2,1)S(1)}, bf16[8,1024,64]{1,2,0:T(8,128)(2,1)}, u32[]{:S(2)}) copy-start(bf16[8,1024,64]{1,2,0:T(8,128)(2,1)} %param.9) | copy-start | bytes 3145732
  15.9 230.1 %all-to-all-start = ((bf16[64,1024,16]{1,2,0:T(8,128)(2,1)}), bf16[64,1024,16]{1,2,0:T(8,128)(2,1)}, u32[]{:S(2)}, u32[]{:S(2)}) async-start(bf16[64,1024,16]{1,2,0:T(8,128)(2,1)} %stack.2), calls=%async_computation | async-start | bytes 4194304 | tf_op jit(solution)/shard_map/all_to_all | solution.py:12
  32.8 66.2 %copy-start.2 = (bf16[64,1024]{1,0:T(8,128)(2,1)S(1)}, bf16[64,1024]{1,0:T(8,128)(2,1)}, u32[]{:S(2)}) copy-start(bf16[64,1024]{1,0:T(8,128)(2,1)} %broadcast_select_fusion) | copy-start | bytes 393220
  32.9 207.4 %all-reduce.4.cloned.1.call-start = ((), (), s32[]{:S(2)}) async-start(), calls=%async_computation.3 | async-start | bytes 131072 | tf_op jit(solution)/shard_map/psum | solution.py:48
  34.7 765.8 %all-reduce.6.cloned.1.call-start = ((), (), s32[]{:S(2)}) async-start(), calls=%async_computation.6 | async-start | bytes 4718592 | tf_op jit(solution)/shard_map/psum | solution.py:100
  246.0 601.3 %reduce-scatter.2.cloned.1.call-start = ((), (), s32[]{:S(2)}) async-start(), calls=%async_computation.2 | async-start | bytes 1179648 | tf_op jit(solution)/shard_map/reduce_scatter | solution.py:50
  246.0 4.0 copy-start.8
  246.0 4.1 copy-start.5
  250.0 1.2 copy-start.6
  802.4 2.6 copy-start.4
  802.4 44.8 %copy-start.1 = (bf16[8,64,1024]{2,1,0:T(8,128)(2,1)S(1)}, bf16[8,64,1024]{2,1,0:T(8,128)(2,1)}, u32[]{:S(2)}) copy-start(bf16[8,64,1024]{2,1,0:T(8,128)(2,1)} %all-gather.3.cloned.1.call-done) | copy-start | bytes 3145732
Sparse Core Ops, SparseCore 0:
  10.0 89.0 all-gather.2
  101.7 52.3 all-gather.4
  157.6 82.5 all-reduce.3
  246.1 554.4 all-reduce.5
  803.2 43.9 reduce-scatter.1
